TPU v7x, 32 devices: a whole 2x2x4 slice. The times are simulated.
32 devices in a mesh: dp: 4 (over z), fsdp: 8 (over y, x, core).
Axes of the slice: x: 2, y: 2, z: 4, core: 2. Of those that a mesh axis runs over, the one named last changes fastest.
Arguments:
- tokens: bfloat16 [32768, 1024], P(('dp', 'fsdp')), may hold values from -6 to 6
- norm_gain: bfloat16 [2, 1024], P(None, ('dp', 'fsdp')), may hold values from 0.5 to 1.5
- norm_bias: bfloat16 [2, 1024], P(None, ('dp', 'fsdp')), may hold values from -1 to 1
- w_qkv: bfloat16 [1024, 3072], P(('dp', 'fsdp')), may hold values from -0.1875 to 0.1875
- attn_bias: bfloat16 [3, 1024], P(None, ('dp', 'fsdp')), may hold values from -1 to 1
- w_attn_out: bfloat16 [1024, 1024], P(('dp', 'fsdp')), may hold values from -0.75 to 0.75
- expert_in: bfloat16 [2, 1024, 4096], P(None, ('dp', 'fsdp')), may hold values from -0.1875 to 0.1875
- expert_in_bias: bfloat16 [2, 4096], P(None, ('dp', 'fsdp')), may hold values from -1 to 1
- expert_out: bfloat16 [2, 4096, 1024], P(None, ('dp', 'fsdp')), may hold values from -0.125 to 0.125
- expert_out_bias: bfloat16 [2, 1024], P(None, ('dp', 'fsdp')), may hold values from -1 to 1
- expert_ids: int32 [32768, 1], P(('dp', 'fsdp')), may hold values from 0 to 1, as said below
- running_load: float32 [2], replicated, may hold values from 0.5 to 1.5
- cotangent: bfloat16 [32768, 1024], P(('dp', 'fsdp')), may hold values from -6 to 6
Outputs:
- block_out: bfloat16 [32768, 1024], P(('dp', 'fsdp'))
- input_grad: float32 [32768, 1024], P(('dp', 'fsdp'))
- norm_gain_grad: float32 [2, 1024], P(None, ('dp', 'fsdp'))
- norm_bias_grad: float32 [2, 1024], P(None, ('dp', 'fsdp'))
- qkv_grad: float32 [1024, 3072], P(('dp', 'fsdp'))
- attn_bias_grad: float32 [3, 1024], P(None, ('dp', 'fsdp'))
- attn_out_grad: float32 [1024, 1024], P(('dp', 'fsdp'))
- expert_in_grad: float32 [2, 1024, 4096], P(None, ('dp', 'fsdp'))
- expert_in_bias_grad: float32 [2, 4096], P(None, ('dp', 'fsdp'))
- expert_out_grad: float32 [2, 4096, 1024], P(None, ('dp', 'fsdp'))
- expert_out_bias_grad: float32 [2, 1024], P(None, ('dp', 'fsdp'))
- expert_counts: int32 [2], replicated
- expert_load: float32 [2], replicated
Inputs may be any that keep to these rules, and one draw needn't show every extreme that they name: `expert_ids`: among the tokens of one device no expert is named more than 640 times; in some device's tokens some expert is named exactly 640 times.
All inputs are finite; a program needn't handle non-finite values.
Results may differ from a plain program's by a relative error of at most 0.0095.
Values may be sent and summed in bfloat16 or wider, within the bound.
A program may use at most 448 MiB of HBM per device.

v0:
```python
import functools
import math

import jax
import jax.numpy as jnp
from jax import lax
from jax.experimental import pallas as pl
from jax.experimental.pallas import tpu as pltpu
from jax.sharding import Mesh, PartitionSpec as P

BF16 = jnp.bfloat16
F32 = jnp.float32
MESH_ID = pl.DeviceIdType.MESH

HEAD = 64
MOST = 640
EXPERTS = 2
CHUNKS = 2
CUTS = 4
AHEAD = 1
NORM_EPS = 1e-05
SCORE_SCALE = 0.125
SCALE_LOG2 = SCORE_SCALE * math.log2(math.e)
MASKED = -1e30
BLOCK = 256
MIB = 1 << 20
ALL = slice(None)
HBM = pl.BlockSpec(memory_space=pl.ANY)
VMEM = pl.BlockSpec(memory_space=pltpu.VMEM)


def dot(left, right):
    return lax.dot_general(left, right, (((1,), (0,)), ((), ())), preferred_element_type=F32)


def dot_last(left, right):
    return lax.dot_general(left, right, (((1,), (1,)), ((), ())), preferred_element_type=F32)


def row_stats(values):
    center = values - jnp.mean(values, axis=-1, keepdims=True)
    spread = jnp.mean(center * center, axis=-1, keepdims=True)
    inverse = lax.rsqrt(spread + NORM_EPS)
    return center * inverse, inverse


def as_rows(values, rows):
    if values.dtype == BF16 and values.shape[-2] % 16:
        return values.astype(F32).reshape(rows, values.shape[-1]).astype(BF16)
    return values.reshape(rows, values.shape[-1])


def split_rows(values, shape):
    if values.dtype == BF16 and shape[-2] % 16:
        return values.astype(F32).reshape(shape).astype(BF16)
    return values.reshape(shape)


class Place:
    def __init__(self, nz, nx):
        self.nz, self.nx = nz, nx
        self.bits_z, self.bits_x = nz.bit_length() - 1, nx.bit_length() - 1
        self.z, self.xy, self.core = lax.axis_index("dp"), lax.axis_index("xy"), lax.axis_index("core")
        self.flip_z = [(1 - 2 * lax.rem(lax.div(self.z, 2**k), 2)) * 2**k for k in range(self.bits_z)]
        self.flip_x = [(1 - 2 * lax.rem(lax.div(self.xy, 2**k), 2)) * 2**k for k in range(self.bits_x)]

    def step_x(self, k, core=None):
        core = self.core if core is None else core
        return (1 - core) * self.flip_x[k] + core * self.flip_x[self.bits_x - 1 - k]

    def span_x(self, which, core=None):
        return self.xy + sum(self.step_x(k, core) for k in range(self.bits_x) if which >> k & 1)

    def span_z(self, which):
        return self.z + sum(self.flip_z[k] for k in range(self.bits_z) if which >> k & 1)

    def partners(self):
        found = [(self.z + flip, self.xy, self.core) for flip in self.flip_z]
        found += [(self.z, self.xy + flip, self.core) for flip in self.flip_x]
        return found + [self.sibling()]

    def sibling(self):
        return (self.z, self.xy, 1 - self.core)

    def barrier(self):
        semaphore = pltpu.get_barrier_semaphore()
        partners = self.partners()
        for partner in partners:
            pl.semaphore_signal(semaphore, inc=1, device_id=partner, device_id_type=MESH_ID)
        pl.semaphore_wait(semaphore, len(partners))


class Copies:
    def __init__(self, send, recv, near):
        self.send, self.recv, self.near = send, recv, near
        self.far_names, self.near_names = {}, {}

    def far(self, name, src, dst, device):
        i = self.far_names.setdefault(name, len(self.far_names))
        return pltpu.make_async_remote_copy(
            src_ref=src, dst_ref=dst, send_sem=self.send.at[i], recv_sem=self.recv.at[i],
            device_id=device, device_id_type=MESH_ID,
        )

    def local(self, name, src, dst, slot=None):
        if slot is not None:
            self.near_names.setdefault((name, 0), len(self.near_names))
            self.near_names.setdefault((name, 1), len(self.near_names))
            return pltpu.make_async_copy(src, dst, self.near.at[self.near_names[name, 0] + slot])
        i = self.near_names.setdefault(name, len(self.near_names))
        return pltpu.make_async_copy(src, dst, self.near.at[i])


def semaphores(far, near):
    return [
        pltpu.SemaphoreType.DMA((far,)),
        pltpu.SemaphoreType.DMA((far,)),
        pltpu.SemaphoreType.DMA((near,)),
    ]


class Stream:
    def __init__(self, pieces):
        self.pieces = pieces
        self.begun = {}

    def advance(self, piece, stage):
        if stage > 0:
            self.finish(piece, stage - 1)
        self.begin(piece, stage)
        self.begun[piece] = stage

    def last(self, piece):
        return self.stages(self.pieces[piece]) - 1


class Schedule:
    def __init__(self, place):
        self.plan = PLAN if (place.nz, place.nx) == PLAN_MESH else None
        self.streams = {}

    def at(self, point):
        for item in (self.plan or {}).get(point, ()):
            self.streams[item // 1000].advance(item % 1000 // 10, item % 10)

    def in_loop(self, i, name, count):
        for k in range(count):
            if (self.plan or {}).get(f"{name}{k}"):
                @pl.when(i == k)
                def _(k=k):
                    self.at(f"{name}{k}")

    def need(self, point, stream, pieces):
        self.at(point)
        if self.plan is None:
            most = max(stream.last(piece) for piece in pieces)
            for now in range(len(pieces) + most):
                for stage in range(most, -1, -1):
                    if 0 <= now - stage < len(pieces):
                        piece = pieces[now - stage]
                        if stream.begun.get(piece, -1) < stage <= stream.last(piece):
                            stream.advance(piece, stage)
        for piece in pieces:
            stream.finish(piece, stream.last(piece))

    def force(self, stream, piece, stage):
        if self.plan is None:
            for now in range(stream.begun.get(piece, -1) + 1, stage + 1):
                stream.advance(piece, now)


class Gather(Stream):
    def __init__(self, name, place, copies, pieces):
        super().__init__(pieces)
        self.name, self.place, self.made = name, place, copies

    def stages(self, piece):
        return self.place.bits_z + self.place.bits_x + (piece[2] is not None)

    def copies(self, piece, stage):
        place = self.place
        order, region, to_sibling = self.pieces[piece]
        step_z = stage if order == "z" else stage - place.bits_x
        step_x = stage - place.bits_z if order == "z" else stage
        found = []
        if stage == place.bits_z + place.bits_x:
            found += [(ref, place.sibling()) for ref in to_sibling]
        elif 0 <= step_z < place.bits_z:
            bit = place.bits_z - 1 - step_z
            device = (place.z + place.flip_z[bit], place.xy, place.core)
            for held in range(2**step_z):
                held_xy = place.xy if order == "z" else ALL
                found += [(ref, device) for ref in region(place.span_z(held << (bit + 1)), held_xy)]
        else:
            device = (place.z, place.xy + place.step_x(step_x), place.core)
            for held in range(2**step_x):
                held_z = ALL if order == "z" else place.z
                found += [(ref, device) for ref in region(held_z, place.span_x(held))]
        return [
            self.made.far((self.name, piece, stage, i), ref, ref, device) for i, (ref, device) in enumerate(found)
        ]

    def begin(self, piece, stage):
        for copy in self.copies(piece, stage):
            copy.start()

    def finish(self, piece, stage):
        for copy in self.copies(piece, stage):
            copy.wait()


def add_up(total, landed):
    if len(total.shape) > 3:
        @pl.loop(0, total.shape[0])
        def _(i):
            add_up(total.at[i], landed.at[i])
    else:
        total[...] = (total[...].astype(F32) + landed[...].astype(F32)).astype(BF16)


class Reduce(Stream):
    def __init__(self, name, place, copies, pieces):
        super().__init__(pieces)
        self.name, self.place, self.made = name, place, copies

    def stages(self, piece):
        return self.place.bits_z + self.place.bits_x + 1

    def plan(self, piece, stage):
        place = self.place
        nx, bits_x, bits_z = place.nx, place.bits_x, place.bits_z
        pair = isinstance(self.pieces[piece], PairPiece)
        if pair:
            order, landing, acc = self.pieces[piece].order, self.pieces[piece].landing, self.pieces[piece].acc
            first, landed = False, landing[stage - 1]
            step = stage - 1
        else:
            order, landing, spare, source, _, _ = self.pieces[piece]
            acc, first, landed, step = landing[0], stage == 0, landing[stage], stage
        far, near, sums = [], [], []
        step_x = step if order == "z" else step - bits_z
        step_z = step - bits_x if order == "z" else step
        if 0 <= step_x < bits_x:
            k = bits_x - 1 - step_x
            device = (place.z, place.xy + place.step_x(k), place.core)
            for j in range(2**k):
                if first:
                    far.append((source(ALL, place.span_x(2**k + j)), acc.at[j], device))
                    near.append((source(ALL, place.span_x(j)), spare.at[j]))
                    sums.append((acc.at[j], spare.at[j]))
                elif order == "x":
                    at_z = place.z if pair else 0
                    far.append((acc.at[at_z, place.span_x(2**k + j)], landed.at[j], device))
                    sums.append((acc.at[at_z, place.span_x(j)], landed.at[j]))
                elif pair:
                    far.append((acc.at[:, place.span_x(2**k + j)], landed.at[j], device))
                    sums += [(acc.at[i, place.span_x(j)], landed.at[j, i]) for i in range(place.nz)]
                else:
                    far.append((acc.at[2**k + j], landed.at[j], device))
                    sums.append((acc.at[j], landed.at[j]))
        else:
            bit = step_z
            device = (place.z + place.flip_z[bit], place.xy, place.core)
            for s in range(2 ** (bits_z - 1 - bit)):
                upper = s << (bit + 1)
                if first:
                    far.append((source(place.span_z(upper + 1), ALL), acc.at[s], device))
                    near.append((source(place.span_z(upper), ALL), spare.at[s]))
                    sums.append((acc.at[s], spare.at[s]))
                elif order == "z":
                    at_xy = place.xy if pair else None
                    send, keep = place.span_z(upper + 2**bit), place.span_z(upper)
                    far.append((acc.at[send, at_xy] if pair else acc.at[0, send], landed.at[s], device))
                    sums.append((acc.at[keep, at_xy] if pair else acc.at[0, keep], landed.at[s]))
                else:
                    send = place.span_z(upper + 2**bit) if pair else (upper + 2**bit) // 2
                    keep = place.span_z(upper) if pair else upper // 2
                    far.append((acc.at[send], landed.at[s], device))
                    sums.append((acc.at[keep], landed.at[s]))
        return far, near, sums

    def made_copies(self, piece, stage, far, near):
        made = [
            self.made.far((self.name, piece, stage, i), src, dst, device) for i, (src, dst, device) in enumerate(far)
        ]
        return made + [self.made.local((self.name, piece, stage, i), src, dst) for i, (src, dst) in enumerate(near)]

    def deliver(self, piece, begin):
        place, core = self.place, self.place.core
        order, landing, _, _, target, owner = self.pieces[piece]
        mine = landing[0].at[0, place.z if order == "z" else place.xy]
        name = (self.name, piece, "last")

        def there(part):
            return self.made.far(name, part, target(core), place.sibling())

        def here(part):
            return self.made.local(name, part, target(core))

        if owner == "both":
            for copy in (there(mine.at[1 - core]), here(mine.at[core])):
                copy.start() if begin else copy.wait()
            return

        @pl.when(core == owner)
        def _():
            if begin:
                here(mine).start()
            else:
                here(mine).wait()
                there(mine).wait_recv()

        @pl.when(core != owner)
        def _():
            there(mine).start() if begin else there(mine).wait_send()

    def to_pair(self, piece):
        item, place = self.pieces[piece], self.place
        return self.made.far((self.name, piece, "pair"), item.source(1 - place.core), item.landed, place.sibling())

    def begin(self, piece, stage):
        pair = isinstance(self.pieces[piece], PairPiece)
        if pair and stage == 0:
            self.to_pair(piece).start()
            return
        if not pair and stage == self.stages(self.pieces[piece]) - 1:
            self.deliver(piece, True)
            return
        far, near, _ = self.plan(piece, stage)
        for copy in self.made_copies(piece, stage, far, near):
            copy.start()

    def finish(self, piece, stage):
        item, final = self.pieces[piece], stage == self.stages(self.pieces[piece]) - 1
        pair = isinstance(item, PairPiece)
        if pair and stage == 0:
            self.to_pair(piece).wait()
            here = self.made.local((self.name, piece, "pair"), item.landed, item.acc)
            here.start()
            here.wait()
            add_up(item.acc, item.source(self.place.core))
            return
        if final and not pair:
            self.deliver(piece, False)
            return
        far, near, sums = self.plan(piece, stage)
        for copy in self.made_copies(piece, stage, far, near):
            copy.wait()
        for total, landed in sums:
            add_up(total, landed)
        if final:
            here = self.made.local((self.name, piece, "last"), item.acc.at[self.place.z, self.place.xy], item.target)
            here.start()
            here.wait()


class PairPiece:
    def __init__(self, order, source, landed, acc, landing, target):
        self.order, self.source, self.landed, self.acc = order, source, landed, acc
        self.landing, self.target = landing, target


def landing_shapes(nz, nx, tail, order):
    bits_z, bits_x = nz.bit_length() - 1, nx.bit_length() - 1
    if order == "z":
        return [(2**k, nz) + tail for k in reversed(range(bits_x))] + [
            (2 ** (bits_z - 1 - bit),) + tail for bit in range(bits_z)
        ]
    return [(2 ** (bits_z - 1 - bit), nx) + tail for bit in range(bits_z)] + [
        (2**k,) + tail for k in reversed(range(bits_x))
    ]


class Total:
    def __init__(self, place, copies, terms, landing):
        self.place, self.made, self.terms, self.landing = place, copies, terms, landing
        self.stages = len(place.partners())

    def copy(self, stage):
        device = self.place.partners()[stage]
        return self.made.far(("total", stage), self.terms.at[stage % 2], self.landing.at[stage], device)

    def begin(self, stage):
        self.copy(stage).start()

    def finish(self, stage):
        self.copy(stage).wait()
        self.terms[(stage + 1) % 2] = self.terms[stage % 2] + self.landing[stage]


def one_hot(slots, count):
    rows = lax.broadcasted_iota(jnp.int32, (count, slots.shape[1]), 0)
    return jnp.where(rows == slots, 1.0, 0.0).astype(BF16)


def pick_rows(picked, slots, values):
    picked[...] = dot(one_hot(slots, picked.shape[0]), values).astype(BF16)


def find_slots(slots, ids_ref, core):
    n = ids_ref.shape[1]
    ids = ids_ref[...]
    second = jnp.where(ids == 1, 1.0, 0.0)
    earlier = lax.broadcasted_iota(jnp.int32, (n, n), 0) <= lax.broadcasted_iota(jnp.int32, (n, n), 1)
    before = dot(
        jnp.broadcast_to(second, (16, n)).astype(BF16), jnp.where(earlier, 1.0, 0.0).astype(BF16)
    )[0:1].astype(jnp.int32)
    rank = jnp.where(ids == 1, before - 1, lax.broadcasted_iota(jnp.int32, (1, n), 1) - before)
    own = ids == core
    slots[0:1, :] = jnp.where(own, rank, -1)
    slots[1:2, :] = jnp.where(own, -1, rank)
    slots[2:8, :] = jnp.full((6, n), -1, jnp.int32)
    return jnp.sum(second, axis=1, keepdims=True)


GAIN, SHIFT, ATTN_BIAS, OUT_BIAS, IN_BIAS, DIGITS = 0, 2, 4, 7, 9, 11


def pack_small(small, refs, count_second):
    small[...] = jnp.zeros_like(small)
    for row, ref in zip((GAIN, SHIFT, ATTN_BIAS, OUT_BIAS, IN_BIAS), refs):
        count, share = ref.shape
        small[row : row + count, :share] = ref[...].astype(F32)
    high = jnp.floor(count_second * (1 / 32))
    lane = lax.broadcasted_iota(jnp.int32, (1, 128), 1)
    small[DIGITS : DIGITS + 1, :] = jnp.where(lane == 0, high, jnp.where(lane == 1, count_second - 32 * high, 0.0))


def spread(shares, length, share, place_of, first=0):
    devices = shares.shape[0]
    lanes = lax.broadcasted_iota(jnp.int32, (128, length), 1)
    chosen = lax.rem(lanes, share) + first == lax.broadcasted_iota(jnp.int32, (128, length), 0)
    repeat = jnp.where(chosen, 1.0, 0.0)
    copies = dot(shares, repeat.astype(BF16))
    lanes = lax.broadcasted_iota(jnp.int32, (devices, length), 1)
    device = lax.broadcasted_iota(jnp.int32, (devices, length), 0)
    return jnp.sum(jnp.where(lax.div(lanes, share) == place_of(device), copies, 0.0), axis=0, keepdims=True)


def unpack_small(small_full, core, d, share, hidden_share, vectors, in_bias, out_bias, counts):
    nz, nx = small_full.shape[:2]
    devices = nz * nx * 2
    found = small_full[...].astype(F32).reshape(devices, 16, 128)

    def rows(row):
        return found[:, row, :].astype(BF16)

    def vector(shares):
        return spread(shares, d, share, lambda device: device)

    vectors[...] = jnp.zeros_like(vectors)
    for line, row, part in (
        (0, GAIN, 0), (0, GAIN + 1, 1), (0, ATTN_BIAS + 2, 2), (1, SHIFT, 0), (1, SHIFT + 1, 1),
        (2, ATTN_BIAS, 0), (2, ATTN_BIAS + 1, 2),
    ):
        vectors[line : line + 1, part * d : (part + 1) * d] = vector(rows(row))

    def of_expert(row):
        return jnp.where(core == 0, rows(row), rows(row + 1))

    out_bias[0:1, :] = vector(of_expert(OUT_BIAS))
    cut = hidden_share // CUTS
    for chunk in range(CHUNKS):
        for i in range(CUTS):
            in_bias[chunk * CUTS + i, 0:1, :] = spread(
                of_expert(IN_BIAS), in_bias.shape[2], cut,
                lambda device: jnp.where(lax.rem(device, 2) == chunk, lax.div(device, 2), -1), i * cut,
            )
    counts[...] = jnp.broadcast_to(jnp.sum(found[:, DIGITS, :], axis=0, keepdims=True), counts.shape)


def attend_pair(qkv, head, attended, log_total):
    n, d = attended.shape
    low = lax.broadcasted_iota(jnp.int32, (n, 128), 1) < HEAD
    one, zero = jnp.ones((), BF16), jnp.zeros((), BF16)
    query = qkv[:, pl.ds(pl.multiple_of(head * 128, 128), 128)]
    key = qkv[:, pl.ds(pl.multiple_of(d + head * 128, 128), 128)]
    value = qkv[:, pl.ds(pl.multiple_of(2 * d + head * 128, 128), 128)]
    values = [jnp.where(low, value, one), jnp.where(low, one, value)]
    queries = [jnp.where(low, query, zero), jnp.where(low, zero, query)]
    low = low[:BLOCK]
    allowed = lax.broadcasted_iota(jnp.int32, (BLOCK, BLOCK), 1) <= lax.broadcasted_iota(
        jnp.int32, (BLOCK, BLOCK), 0
    )
    for i in range(n // BLOCK):
        first, end = i * BLOCK, (i + 1) * BLOCK
        found = []
        for j in range(2):
            near = jnp.where(allowed, dot_last(queries[j][first:end], key[first:end]), MASKED)
            top = jnp.max(near, axis=-1, keepdims=True)
            if i:
                far = dot_last(queries[j][first:end], key[:first])
                top = jnp.maximum(top, jnp.max(far, axis=-1, keepdims=True))
            top = top * SCALE_LOG2
            out = dot(jnp.exp2(near * SCALE_LOG2 - top).astype(BF16), values[j][first:end])
            if i:
                out = out + dot(jnp.exp2(far * SCALE_LOG2 - top).astype(BF16), values[j][:first])
            found.append((out, top))
        (out_a, top_a), (out_b, top_b) = found
        total = pltpu.roll(jnp.where(low, out_b, out_a), HEAD, axis=1)
        attended[first:end, pl.ds(pl.multiple_of(head * 128, 128), 128)] = (
            jnp.where(low, out_a, out_b) / total
        ).astype(BF16)
        logs = (jnp.where(low, top_a, top_b) + jnp.log2(total)).T
        log_total[head, 0:1, first:end] = logs[0:1]
        log_total[head, 1:2, first:end] = logs[HEAD : HEAD + 1]


def gelu_and_slope(values):
    root = math.sqrt(2 / math.pi)
    cube = 0.044715
    square = values * values
    bent = jnp.tanh(values * (root + root * cube * square))
    half = 0.5 * (1 + bent)
    slope = half + 0.5 * values * (1 - bent * bent) * (root + 3 * root * cube * square)
    return values * half, slope


def norm_backward(values, gain, grad):
    scaled, inverse = row_stats(values)
    grad_scaled = grad * gain
    mean = jnp.mean(grad_scaled, axis=-1, keepdims=True)
    along = jnp.mean(grad_scaled * scaled, axis=-1, keepdims=True)
    term = inverse * (grad_scaled - mean - scaled * along)
    return term, jnp.sum(grad * scaled, axis=0, keepdims=True), jnp.sum(grad, axis=0, keepdims=True)


def attend_pair_backward(qkv, head, attended, grad, log_total, projected, turned):
    n, d = attended.shape
    low = lax.broadcasted_iota(jnp.int32, (n, 128), 1) < HEAD
    zero = jnp.zeros((), BF16)

    def columns(part):
        return pl.ds(pl.multiple_of(part * d + head * 128, 128), 128)

    query, key, value = (qkv[:, columns(part)] for part in range(3))
    grad = grad[:, columns(0)]
    product = (attended[:, columns(0)].astype(F32) * grad.astype(F32)).T
    inner = [jnp.sum(product[j * HEAD : (j + 1) * HEAD], axis=0, keepdims=True) for j in range(2)]
    logs = [log_total[head, j : j + 1, :] for j in range(2)]
    key_turned = key.T
    keys = [jnp.where(low, key, zero), jnp.where(low, zero, key)]
    values = [jnp.where(low, value, zero), jnp.where(low, zero, value)]
    low = low[:BLOCK]
    allowed = lax.broadcasted_iota(jnp.int32, (BLOCK, BLOCK), 0) <= lax.broadcasted_iota(
        jnp.int32, (BLOCK, BLOCK), 1
    )
    for i in range(n // BLOCK):
        first, end = i * BLOCK, (i + 1) * BLOCK
        found = []
        for j in range(2):
            grad_key = grad_value = 0.0
            for start, stop in ((first, end), (end, n)):
                if start == stop:
                    continue
                scores = dot_last(keys[j][first:end], query[start:stop])
                weights = jnp.exp2(scores * SCALE_LOG2 - logs[j][:, start:stop])
                if start == first:
                    weights = jnp.where(allowed, weights, 0.0)
                grad_weights = dot_last(values[j][first:end], grad[start:stop])
                grad_scores = (weights * (grad_weights - inner[j][:, start:stop])).astype(BF16)
                grad_value = grad_value + dot(weights.astype(BF16), grad[start:stop])
                grad_key = grad_key + dot(grad_scores, query[start:stop])
                part = dot(key_turned[j * HEAD : (j + 1) * HEAD, first:end], grad_scores)
                if i == 0:
                    turned[j * HEAD : (j + 1) * HEAD, start:stop] = part
                else:
                    turned[j * HEAD : (j + 1) * HEAD, start:stop] += part
            found.append((grad_key, grad_value))
        (key_a, value_a), (key_b, value_b) = found
        projected[first:end, columns(1)] = (jnp.where(low, key_a, key_b) * SCORE_SCALE).astype(BF16)
        projected[first:end, columns(2)] = jnp.where(low, value_a, value_b).astype(BF16)
    projected[:, columns(0)] = (turned[...].T * SCORE_SCALE).astype(BF16)


PLAN_MESH = (4, 4)
GATHER_ACROSS = (7, 11, 15, 17)
REDUCE_ACROSS = (7, 8, 14)
PLAN = {
    "s0": (0,),
    "s1": (10, 70, 110, 170, 150,),
    "s2": (1,),
    "s3": (20, 71,),
    "w0": (111, 171, 2, 11, 21, 151, 40, 12, 80, 3, 30, 41, 22, 81, 13, 31, 4, 50, 42, 90,),
    "w1": (82, 60, 51, 23, 14, 91, 100,),
    "w2": (43, 61, 120, 83, 101, 24, 72, 32,),
    "q0": (52, 121, 92,),
    "q1": (33, 112,),
    "q3": (53,),
    "h0": (73,),
    "h1": (34, 93,),
    "h2": (62,),
    "h3": (102, 113,),
    "h4": (122,),
    "h5": (63,),
    "h6": (103, 160,),
    "h7": (130,),
    "o0": (123, 161,),
    "o1": (131,),
    "o2": (140,),
    "o3": (162, 180,),
    "d0": (132, 172,),
    "e0": (163,),
    "t0.0": (133,),
    "t1.0": (141,),
    "t2.0": (181,),
    "t0.1": (142, 173,),
    "t1.1": (182,),
    "t2.1": (143,),
    "t0.2": (183, 190,),
    "t1.2": (152,),
    "t2.2": (1000,),
    "t1.3": (1040,),
    "t2.3": (191,),
    "t0.4": (153, 1001,),
    "t1.4": (192,),
    "t2.4": (1041,),
    "t0.5": (193, 1002,),
    "t1.5": (1042, 1010,),
    "t2.5": (1070,),
    "t0.6": (1050,),
    "t2.6": (1003, 1011,),
    "t0.7": (1043, 1051,),
    "t1.7": (1004, 1012, 1020,),
    "t2.7": (1044, 1052, 1060,),
    "x": (1071,),
    "b0": (1021,),
    "b1": (1013, 1061,),
    "b2": (1053, 1030,),
    "b3": (1014, 1022, 1072, 1120, 1062,),
    "wo2": (1054, 1190, 1080,),
    "a0": (1031,),
    "a1": (1023, 1073, 1121,),
    "a2": (1063, 1074, 1090,),
    "a3": (1024, 1032, 1064, 1130,),
    "a4": (1081, 1091,),
    "a5": (1131,),
    "a6": (1033, 1100,),
    "a7": (1122, 1150,),
    "free": (1034, 1092, 1082, 1132,),
    "p0": (1123, 1101, 1160, 1110, 1140,),
    "p1": (1170, 1191,),
    "p2": (1124, 1180,),
    "i0": (1093,),
    "i1": (1083, 1133, 1111,),
    "i2": (1192, 1102, 1084, 1094, 1151, 1141,),
    "i3": (1134, 1161,),
    "m0": (1171,),
    "m1": (1193,),
    "m2": (1103, 1142, 1162, 1112,),
    "m3": (1194, 1172,),
    "m4": (1104, 1143, 1113, 1181, 1152,),
    "end": (1144, 1163, 1114, 1173, 1153, 1182, 1164, 1174, 1154, 1183, 1184,),
}


def gathered_columns(pieces):
    found, at = None, 0
    for values, first, lanes in pieces:
        moved = pltpu.roll(values, (at - first) % 128, axis=values.ndim - 1) if at != first else values
        lane = lax.broadcasted_iota(jnp.int32, values.shape, values.ndim - 1)
        found = moved if found is None else jnp.where(lane >= at, moved, found)
        at += lanes
    return found


def whole_tiles(hidden_share):
    return hidden_share % 128 == 0


def split_columns(whole, parts, hidden_share):
    width = parts.shape[-1]
    cut = hidden_share // CUTS
    if not whole_tiles(hidden_share):
        for chunk in range(CHUNKS):
            parts[chunk] = whole[:, :, chunk * width : (chunk + 1) * width]
        return
    for expert in range(whole.shape[0]):
        for at in range(0, CHUNKS * width, 128):
            chunk, k, chip = at // width, at % width // (width // CUTS), at % (width // CUTS) // cut
            pieces = []
            for i in range(128 // cut):
                first = ((chip + i) * CHUNKS + chunk) * hidden_share + k * cut
                block = whole[expert, :, first // 128 * 128 : first // 128 * 128 + 128].astype(F32)
                pieces.append((block, first % 128, cut))
            parts[chunk, expert, :, at % width : at % width + 128] = gathered_columns(pieces).astype(BF16)


def join_columns(parts, whole, hidden_share):
    width = parts.shape[-1]
    cut = hidden_share // CUTS
    if not whole_tiles(hidden_share):
        for chunk in range(CHUNKS):
            whole[:, :, chunk * width : (chunk + 1) * width] = parts[chunk].astype(F32)
        return
    for expert in range(whole.shape[0]):
        for at in range(0, CHUNKS * width, 128):
            chip, chunk = at // hidden_share // CHUNKS, at // hidden_share % CHUNKS
            pieces = []
            for k in range(at % hidden_share // cut, at % hidden_share // cut + 128 // cut):
                first = k * (width // CUTS) + chip * cut
                block = parts[chunk, expert, :, first // 128 * 128 : first // 128 * 128 + 128].astype(F32)
                pieces.append((block, first % 128, cut))
            whole[expert, :, at : at + 128] = gathered_columns(pieces)


def block_kernel(nz, nx, tokens, cotangent, ids, small, w_qkv, w_out, in_shard, hidden_own):
    n, d = tokens.shape
    heads = d // 128
    depth = w_qkv.shape[0]
    share = small[0].shape[1]
    hidden_share = hidden_own.shape[1]
    width = in_shard.shape[2] // CHUNKS
    tile = width // CUTS
    tiles = CUTS
    count = 2 * MOST
    cut = width // CUTS
    hidden_cut = hidden_share // CUTS
    in_tail, hidden_tail = (2, depth, cut), (hidden_cut, d)
    small_rows = 10 + EXPERTS * CHUNKS * (width // d)
    small_rows += -small_rows % 8

    def bf16(*shape):
        return jax.ShapeDtypeStruct(shape, BF16)

    def f32(*shape):
        return jax.ShapeDtypeStruct(shape, F32)

    outputs = dict(
        block_out=bf16(n, d),
        input_grad=f32(n, d),
        qkv_sum=bf16(depth, 3 * d),
        wo_sum=bf16(depth, d),
        in_sum=bf16(CHUNKS, EXPERTS, depth, width),
        hidden_sum=bf16(EXPERTS, hidden_share, d),
        pair_terms=bf16(4, nz, nx, depth, d),
        qkv_full=bf16(nz, nx, 2, depth, 3 * d),
        wo_full=bf16(nz, nx, 2, depth, d),
        grad_rows=bf16(2, MOST, d),
        rows=bf16(2, MOST, d),
        made_rows=bf16(2, MOST, d),
        back_rows=bf16(2, MOST, d),
        in_full=bf16(CHUNKS, nz, nx, 2, depth, width),
        hidden_full=bf16(CHUNKS, nz, nx, hidden_share, d),
        in_terms=bf16(CHUNKS, nz, nx, 2, depth, width),
        hidden_terms=bf16(CHUNKS, nz, nx, hidden_share, d),
        normed=bf16(n, d),
        qkv=bf16(n, 3 * d),
        attended=bf16(n, d),
        logs=f32(heads, 8, n),
        residual=f32(n, d),
    )
    small_outputs = dict(small_sum=f32(small_rows, d), counts=f32(8, 128))

    gather_order = ["x" if piece in GATHER_ACROSS and nz == nx else "z" for piece in range(20)]
    reduce_order = ["x" if piece in REDUCE_ACROSS and nz == nx else "z" for piece in range(20)]
    landings = []
    for chunk in range(CHUNKS):
        for i in range(2 * CUTS):
            tail = in_tail if i < CUTS else hidden_tail
            landings.append(landing_shapes(nz, nx, tail, reduce_order[chunk * 2 * CUTS + i]))
    per_piece = len(landings[0])
    landing_scratch = [pltpu.VMEM(shape, BF16) for shapes in landings for shape in shapes]
    spares = [
        pltpu.VMEM(landing_shapes(nz, nx, tail, order)[0], BF16) for tail in (in_tail, hidden_tail) for order in "zx"
    ]
    partners = nz.bit_length() - 1 + nx.bit_length() - 1 + 1

    names = list(outputs) + list(small_outputs)

    def kernel(*refs):
        (
            tokens_hbm, cot_hbm, ids_ref, gain_ref, shift_ref, attn_bias_ref, out_bias_ref, in_bias_ref,
            qkv_own, wo_own, in_shard, hidden_own,
        ) = refs[:12]
        out = dict(zip(names, refs[12 : 12 + len(names)]))
        rest = refs[12 + len(names) :]
        slots, small_own, small_full, in_bias, out_bias, bias_sums, vectors, terms, terms_landing, free = rest[:10]
        spare = rest[10:14]
        landing = rest[14 : 14 + len(landing_scratch)]
        made = Copies(*rest[14 + len(landing_scratch) :])

        place = Place(nz, nx)
        z, xy, core = place.z, place.xy, place.core
        sums = terms.at[0]
        total = Total(place, made, terms, terms_landing)

        def columns_of(ref, part):
            return lambda zs, xs: [ref.at[zs, xs, core, :, pl.ds(part * d, d)]]

        def with_small(zs, xs):
            return [out["qkv_full"].at[zs, xs, core, :, pl.ds(2 * d, d)], small_full.at[zs, xs, core]]

        regions = [columns_of(out["qkv_full"], 0), columns_of(out["qkv_full"], 1), with_small, columns_of(out["wo_full"], 0)]
        gathered = [(order, region, region(ALL, ALL)) for order, region in zip(gather_order, regions)]
        for chunk in range(CHUNKS):
            for i in range(CUTS):
                at_columns = pl.ds(i * cut, cut)
                gathered.append(
                    (gather_order[len(gathered)], lambda zs, xs, c=chunk, s=at_columns: [out["in_full"].at[c, zs, xs, :, :, s]], None)
                )
            for i in range(CUTS):
                at_rows = pl.ds(i * hidden_cut, hidden_cut)
                gathered.append(
                    (gather_order[len(gathered)], lambda zs, xs, c=chunk, s=at_rows: [out["hidden_full"].at[c, zs, xs, s]], None)
                )
        gather = Gather("gather", place, made, gathered)

        pieces = []
        for chunk in range(CHUNKS):
            for i in range(2 * CUTS):
                at = len(pieces)
                order = reduce_order[at]
                mine = landing[at * per_piece : (at + 1) * per_piece]
                spare_now = spare[i // CUTS * 2 + (order == "x")]
                if i < CUTS:
                    at_columns = pl.ds(i * cut, cut)
                    pieces.append(
                        (
                            order, mine, spare_now,
                            lambda zs, xs, c=chunk, s=at_columns: out["in_terms"].at[c, zs, xs, :, :, s],
                            lambda expert, c=chunk, s=at_columns: out["in_sum"].at[c, expert, :, s],
                            "both",
                        )
                    )
                else:
                    at_rows = pl.ds((i - CUTS) * hidden_cut, hidden_cut)
                    pieces.append(
                        (
                            order, mine, spare_now,
                            lambda zs, xs, c=chunk, s=at_rows: out["hidden_terms"].at[c, zs, xs, s],
                            lambda expert, s=at_rows: out["hidden_sum"].at[expert, s],
                            chunk,
                        )
                    )
        reduce = Reduce("reduce", place, made, pieces)
        schedule = Schedule(place)
        schedule.streams.update({0: gather, 1: reduce})

        def first_phase(cot, picked, shard, in_own, qkv, wo, hidden):
            def load(name, source, target):
                copy = made.local(("first", name), source, target)
                copy.start()
                return copy

            loads = [load("qkv", qkv_own, qkv), load("wo", wo_own, wo), load("hidden", hidden_own, hidden)]
            load_shard = load("shard", in_shard, shard)
            load_cot = load("cot", cot_hbm, cot)
            place.barrier()
            loads[0].wait()
            near = [load("own qkv", qkv, out["qkv_full"].at[z, xy, core])]
            loads[1].wait()
            near.append(load("own wo", wo, out["wo_full"].at[z, xy, core]))
            for copy in near:
                copy.wait()
            schedule.at("s0")
            loads[2].wait()
            late = [load("own hidden", hidden.at[core], out["hidden_full"].at[core, z, xy])]
            pair = [made.far("pair hidden", hidden.at[1 - core], out["hidden_full"].at[core, z, xy], place.sibling())]
            load_shard.wait()
            split_columns(shard, in_own, hidden_share)
            for chunk in range(CHUNKS):
                target = out["in_full"].at[chunk, z, xy, core]
                late.append(load(("own in", chunk), in_own.at[chunk, core], target))
                pair.append(made.far(("pair in", chunk), in_own.at[chunk, 1 - core], target, place.sibling()))
            for copy in pair:
                copy.start()
            count_second = find_slots(slots, ids_ref, core)
            pack_small(small_own, (gain_ref, shift_ref, attn_bias_ref, out_bias_ref, in_bias_ref), count_second)
            small_full[z, xy, core] = small_own[...].astype(BF16)
            for copy in late + pair:
                copy.wait()
            schedule.at("s1")
            load_cot.wait()
            pick_rows(picked.at[1], slots[1:2, :], cot[...])
            theirs = made.far("grad rows", picked.at[1], out["grad_rows"].at[1], place.sibling())
            theirs.start()
            schedule.at("s2")
            pick_rows(picked.at[0], slots[0:1, :], cot[...])
            mine = made.local("grad rows", picked.at[0], out["grad_rows"].at[0])
            mine.start()
            schedule.at("s3")
            mine.wait()
            theirs.wait()

        pl.run_scoped(
            first_phase,
            pltpu.VMEM((n, d), BF16),
            pltpu.VMEM((2, MOST, d), BF16),
            pltpu.VMEM((EXPERTS, depth, CHUNKS * width), BF16),
            pltpu.VMEM((CHUNKS, EXPERTS, depth, width), BF16),
            pltpu.VMEM((depth, 3 * d), BF16),
            pltpu.VMEM((depth, d), BF16),
            pltpu.VMEM((EXPERTS, hidden_share, d), BF16),
        )

        def forward_phase(tok, w, wo, normed, qkv, attended, logs, residual, normed_two, picked):
            load = made.local("tokens", tokens_hbm, tok)
            load.start()
            loads = []
            for part in range(3):
                schedule.need(f"w{part}", gather, [part])
                at_columns = pl.ds(part * d, d)
                loads.append(
                    made.local(
                        ("w", part), out["qkv_full"].at[:, :, :, :, at_columns], w.at[:, :, :, :, at_columns]
                    )
                )
                loads[-1].start()
            unpack_small(small_full, core, d, share, hidden_share, vectors, in_bias, out_bias, out["counts"])
            load.wait()
            for copy in loads:
                copy.wait()

            @pl.loop(0, n // BLOCK)
            def _(i):
                rows = pl.ds(pl.multiple_of(i * BLOCK, BLOCK), BLOCK)
                scaled, _ = row_stats(tok[rows].astype(F32))
                normed[rows] = (scaled * vectors[0:1, :d] + vectors[1:2, :d]).astype(BF16)
                weight = as_rows(w[...], d)
                qkv[rows] = (dot(normed[rows], weight) + vectors[2:3, :]).astype(BF16)
                schedule.in_loop(i, "q", n // BLOCK)

            saves = [
                made.local("save normed", normed, out["normed"]),
                made.local("save qkv", qkv, out["qkv"]),
            ]
            for save in saves:
                save.start()

            @pl.loop(0, heads)
            def _(head):
                attend_pair(qkv, head, attended, logs)
                schedule.in_loop(head, "h", heads)

            saves += [
                made.local("save attended", attended, out["attended"]),
                made.local("save logs", logs, out["logs"]),
            ]
            for save in saves[2:]:
                save.start()
            schedule.need("wo", gather, [3])
            load_wo = made.local("wo", out["wo_full"], wo)
            load_wo.start()
            load_wo.wait()

            @pl.loop(0, n // BLOCK)
            def _(i):
                rows = pl.ds(pl.multiple_of(i * BLOCK, BLOCK), BLOCK)
                added = dot(attended[rows], as_rows(wo[...], d)) + vectors[0:1, 2 * d :]
                residual[rows] = tok[rows].astype(F32) + added
                scaled, _ = row_stats(residual[rows])
                normed_two[rows] = (scaled * vectors[0:1, d : 2 * d] + vectors[1:2, d : 2 * d]).astype(BF16)
                schedule.in_loop(i, "o", n // BLOCK)


            saves.append(made.local("save residual", residual, out["residual"]))
            saves[-1].start()
            pick_rows(picked.at[1], slots[1:2, :], normed_two[...])
            theirs = made.far("rows", picked.at[1], out["rows"].at[1], place.sibling())
            theirs.start()
            schedule.at("d0")
            pick_rows(picked.at[0], slots[0:1, :], normed_two[...])
            saves.append(made.local("rows", picked.at[0], out["rows"].at[0]))
            saves[-1].start()
            schedule.at("d1")
            for save in saves:
                save.wait()
            theirs.wait()

        pl.run_scoped(
            forward_phase,
            pltpu.VMEM((n, d), BF16),
            pltpu.VMEM((nz, nx, 2, depth, 3 * d), BF16),
            pltpu.VMEM((nz, nx, 2, depth, d), BF16),
            pltpu.VMEM((n, d), BF16),
            pltpu.VMEM((n, 3 * d), BF16),
            pltpu.VMEM((n, d), BF16),
            pltpu.VMEM((heads, 8, n), F32),
            pltpu.VMEM((n, d), F32),
            pltpu.VMEM((n, d), BF16),
            pltpu.VMEM((2, MOST, d), BF16),
        )

        def expert_phase(rows, grads, turned, made_total, back_total, w_in, w_hidden, grad_in, grad_hidden):
            loads = [
                made.local("load rows", out["rows"], rows),
                made.local("load grads", out["grad_rows"], grads),
            ]
            for copy in loads:
                copy.start()

            def cut_rows(t):
                return pl.ds(pl.multiple_of(t * hidden_cut, hidden_cut), hidden_cut)

            def weights(step):
                slot, chunk, t = lax.rem(step, 2), lax.div(step, tiles), lax.rem(step, tiles)
                at_columns = pl.ds(pl.multiple_of(t * tile, tile), tile)
                return [
                    made.local("w in", out["in_full"].at[chunk, :, :, :, :, at_columns], w_in.at[slot]),
                    made.local("w hidden", out["hidden_full"].at[chunk, :, :, cut_rows(t)], w_hidden.at[slot]),
                ]

            def stores(step):
                chunk, t = lax.div(step, tiles), lax.rem(step, tiles)
                at_columns = pl.ds(pl.multiple_of(t * tile, tile), tile)
                return [
                    made.local("store in", grad_in, out["in_terms"].at[chunk, :, :, :, :, at_columns]),
                    made.local("store hidden", grad_hidden, out["hidden_terms"].at[chunk, :, :, cut_rows(t)]),
                ]

            terms[0] = jnp.zeros(terms.shape[1:], F32)
            made_total[...] = jnp.zeros_like(made_total)
            back_total[...] = jnp.zeros_like(back_total)
            for copy in loads:
                copy.wait()
            turned[...] = as_rows(rows[...], count).T
            line = jnp.sum(as_rows(grads[...], count).astype(F32), axis=0, keepdims=True)
            for expert in range(EXPERTS):
                sums[8 + expert : 9 + expert, :] = jnp.where(core == expert, line, 0.0)

            def arrive(step):
                chunk, t = step // tiles, step % tiles
                first = 4 + chunk * 2 * CUTS + t
                schedule.need(f"e{step}", gather, [first, first + CUTS])
                for copy in weights(step):
                    copy.start()

            arrive(0)

            @pl.loop(0, CHUNKS * tiles)
            def _(step):
                slot = lax.rem(step, 2)
                for copy in weights(step):
                    copy.wait()

                def beside(spot):
                    schedule.in_loop(step, f"t{spot}.", CHUNKS * tiles)

                rows_now, grads_now = as_rows(rows[...], count), as_rows(grads[...], count)
                w_in_now = as_rows(w_in[slot], d)
                w_hidden_now = as_rows(w_hidden[slot], tile)
                hidden_pre = dot(rows_now, w_in_now) + in_bias[step, 0:1, :]
                hidden, slope = gelu_and_slope(hidden_pre)
                hidden = hidden.astype(BF16)
                grad_pre = dot_last(grads_now, w_hidden_now) * slope
                bias_sums[step, 0:1, :] = jnp.sum(grad_pre, axis=0, keepdims=True)
                grad_pre = grad_pre.astype(BF16)
                beside(0)
                made_total[...] += dot(hidden, w_hidden_now)
                back_total[...] += dot_last(grad_pre, w_in_now)

                @pl.when(step >= 1)
                def _():
                    for copy in stores(step - 1):
                        copy.wait()

                beside(1)
                for k in range(1, CHUNKS * tiles):
                    @pl.when(step == k - 1)
                    def _(k=k):
                        arrive(k)

                grad_hidden[...] = split_rows(dot(hidden.T, grads_now).astype(BF16), (nz, nx, hidden_cut, d))
                grad_in[...] = split_rows(dot(turned[...], grad_pre).astype(BF16), (nz, nx, 2, depth, tile))
                for copy in stores(step):
                    copy.start()
                beside(2)

            for copy in stores(CHUNKS * tiles - 1):
                copy.wait()

            rows[...] = split_rows((made_total[...] + out_bias[0:1, :]).astype(BF16), (2, MOST, d))
            grads[...] = split_rows(back_total[...].astype(BF16), (2, MOST, d))
            results = []
            for name, source in (("made_rows", rows), ("back_rows", grads)):
                results.append(made.far(name, source.at[1], out[name].at[1], place.sibling()))
                results.append(made.local(name, source.at[0], out[name].at[0]))
            for copy in results:
                copy.start()
            schedule.at("x")
            for copy in results:
                copy.wait()

        pl.run_scoped(
            expert_phase,
            pltpu.VMEM((2, MOST, d), BF16),
            pltpu.VMEM((2, MOST, d), BF16),
            pltpu.VMEM((d, count), BF16),
            pltpu.VMEM((count, d), F32),
            pltpu.VMEM((count, d), F32),
            pltpu.VMEM((2, nz, nx, 2, depth, tile), BF16),
            pltpu.VMEM((2, nz, nx, hidden_cut, d), BF16),
            pltpu.VMEM((nz, nx, 2, depth, tile), BF16),
            pltpu.VMEM((nz, nx, hidden_cut, d), BF16),
        )

        def backward_phase(grad_res, branch, grad_att, att, projected, normed, wide, acc):
            def load(name, source, target):
                copy = made.local(("back", name), source, target)
                copy.start()
                return copy

            late_loads = [load("att", out["attended"], att), load("normed", out["normed"], normed)]

            for i in range(4):
                at = CUTS + i
                columns = pl.ds(i * d, d)
                pieces.append(
                    PairPiece(
                        reduce_order[len(pieces)],
                        lambda which, spot=(1, 2, 0, 0)[i]: wide.at[spot, :, :, which],
                        out["pair_terms"].at[i],
                        acc.at[i],
                        landing[at * per_piece : (at + 1) * per_piece],
                        out["wo_sum"] if i == 3 else out["qkv_sum"].at[:, columns],
                    )
                )

            def residual_phase(made_rows, back_rows, cot, wo, block, slots_turned):
                loads = [
                    load("residual", out["residual"], grad_res),
                    load("made", out["made_rows"], made_rows),
                    load("back", out["back_rows"], back_rows),
                    load("cot", cot_hbm, cot),
                    load("wo", out["wo_full"], wo),
                ]
                slots_turned[...] = slots[...].astype(F32).T
                for copy in loads:
                    copy.wait()

                @pl.loop(0, n // BLOCK)
                def _(i):
                    rows = pl.ds(pl.multiple_of(i * BLOCK, BLOCK), BLOCK)
                    columns = lax.broadcasted_iota(jnp.int32, (BLOCK, MOST), 1).astype(F32)
                    chosen = jnp.concatenate(
                        [
                            jnp.where(columns == slots_turned[rows, k : k + 1], 1.0, 0.0).astype(BF16)
                            for k in range(2)
                        ],
                        axis=1,
                    )
                    values = grad_res[rows]
                    block[rows] = (values + dot(chosen, as_rows(made_rows[...], count))).astype(BF16)
                    grad = dot(chosen, as_rows(back_rows[...], count))
                    term, gain_sum, shift_sum = norm_backward(values, vectors[0:1, d : 2 * d], grad)
                    sums[1:2, :] += gain_sum
                    sums[3:4, :] += shift_sum
                    now = cot[rows].astype(F32) + term
                    grad_res[rows] = now
                    low = now.astype(BF16)
                    branch[rows] = low
                    sums[6:7, :] += jnp.sum(low.astype(F32), axis=0, keepdims=True)
                    grad_att[rows] = dot_last(low, as_rows(wo[...], d)).astype(BF16)
                    schedule.in_loop(i, "b", n // BLOCK)

                load("block", block, out["block_out"]).wait()

            pl.run_scoped(
                residual_phase,
                pltpu.VMEM((2, MOST, d), BF16),
                pltpu.VMEM((2, MOST, d), BF16),
                pltpu.VMEM((n, d), BF16),
                pltpu.VMEM((nz, nx, 2, depth, d), BF16),
                pltpu.VMEM((n, d), BF16),
                pltpu.VMEM((n, 8), F32),
            )
            for copy in late_loads:
                copy.wait()
            wide[0] = split_rows(dot(att[...].T, branch[...]).astype(BF16), wide.shape[1:])
            schedule.at("wo2")

            def attend_phase(qkv, logs, turned):
                loads = [load("qkv", out["qkv"], qkv), load("logs", out["logs"], logs)]
                for copy in loads:
                    copy.wait()

                @pl.loop(0, heads)
                def _(head):
                    attend_pair_backward(qkv, head, att, grad_att, logs, projected, turned)
                    schedule.in_loop(head, "a", heads)

            pl.run_scoped(
                attend_phase,
                pltpu.VMEM((n, 3 * d), BF16),
                pltpu.VMEM((heads, 8, n), F32),
                pltpu.VMEM((128, n), F32),
            )

            schedule.need("free", reduce, range(2 * CUTS))
            senders = place.partners()[:-1]
            for device in senders:
                pl.semaphore_signal(free, inc=1, device_id=device, device_id_type=MESH_ID)

            def input_phase(w, tok):
                loads = [load("w", out["qkv_full"], w), load("tok", tokens_hbm, tok)]
                normed_turned = normed[...].T
                for part in range(3):
                    columns = slice(part * d, (part + 1) * d)
                    wide[(1, 2, 0)[part]] = split_rows(
                        dot(normed_turned, projected[:, columns]).astype(BF16), wide.shape[1:]
                    )
                    if part == 1:
                        pl.semaphore_wait(free, len(senders))
                    schedule.at(f"p{part}")
                    if part == 1:
                        schedule.force(reduce, 19, 1)
                    if part != 1:
                        sums[4 + part // 2 : 5 + part // 2, :] = jnp.sum(
                            projected[:, columns].astype(F32), axis=0, keepdims=True
                        )
                for copy in loads:
                    copy.wait()

                @pl.loop(0, n // BLOCK)
                def _(i):
                    rows = pl.ds(pl.multiple_of(i * BLOCK, BLOCK), BLOCK)
                    grad = dot_last(projected[rows], as_rows(w[...], d))
                    term, gain_sum, shift_sum = norm_backward(tok[rows].astype(F32), vectors[0:1, :d], grad)
                    grad_res[rows] += term
                    sums[0:1, :] += gain_sum
                    sums[2:3, :] += shift_sum
                    schedule.in_loop(i, "i", n // BLOCK)

                save = load("input_grad", grad_res, out["input_grad"])
                lines = width // d
                for step in range(CHUNKS * tiles):
                    first = (step % tiles) * tile
                    for expert in range(EXPERTS):
                        row = 10 + expert * CHUNKS * lines + step // tiles * lines + first // d
                        sums[row : row + 1, first % d : first % d + tile] = jnp.where(
                            core == expert, bias_sums[step, 0:1, :], 0.0
                        )
                for stage in range(total.stages):
                    total.begin(stage)
                    schedule.at(f"m{stage}")
                    total.finish(stage)
                out["small_sum"][...] = terms[total.stages % 2]
                schedule.need("end", reduce, range(2 * CUTS, len(pieces)))
                save.wait()

            pl.run_scoped(
                input_phase, pltpu.VMEM((nz, nx, 2, depth, 3 * d), BF16), pltpu.VMEM((n, d), BF16)
            )

        pl.run_scoped(
            backward_phase,
            pltpu.VMEM((n, d), F32),
            pltpu.VMEM((n, d), BF16),
            pltpu.VMEM((n, d), BF16),
            pltpu.VMEM((n, d), BF16),
            pltpu.VMEM((n, 3 * d), BF16),
            pltpu.VMEM((n, d), BF16),
            pltpu.VMEM((3, nz, nx, 2, depth, d), BF16),
            pltpu.VMEM((4, nz, nx, depth, d), BF16),
        )

    exchanged = nz + nx
    results = pl.pallas_call(
        kernel,
        out_shape=list(outputs.values()) + list(small_outputs.values()),
        in_specs=[HBM, HBM] + [VMEM] * 6 + [HBM] * 4,
        out_specs=[HBM] * len(outputs) + [VMEM] * len(small_outputs),
        scratch_shapes=[
            pltpu.VMEM((8, n), jnp.int32),
            pltpu.VMEM((16, 128), F32),
            pltpu.VMEM((nz, nx, 2, 16, 128), BF16),
            pltpu.VMEM((CHUNKS * tiles, 8, tile), F32),
            pltpu.VMEM((8, d), F32),
            pltpu.VMEM((CHUNKS * tiles, 8, tile), F32),
            pltpu.VMEM((8, 3 * d), F32),
            pltpu.VMEM((2, small_rows, d), F32),
            pltpu.VMEM((partners, small_rows, d), F32),
            pltpu.SemaphoreType.REGULAR,
            *spares,
            *landing_scratch,
            *semaphores(40 * exchanged + 48, 16 * (max(nx, nz) // 2 + 2) + 56),
        ],
        compiler_params=pltpu.CompilerParams(
            collective_id=1, has_side_effects=True, vmem_limit_bytes=64 * MIB - 64 * 1024
        ),
        name="block",
    )(tokens, cotangent, ids, *small, w_qkv, w_out, in_shard, hidden_own)
    return dict(zip(names, results))


PARTS = 4


def result_kernel(nz, nx, block, running_load, share, hidden_share):
    devices = nz * nx * 2
    n, d = block["block_out"].shape
    depth, width = block["in_sum"].shape[2:]
    lines = width // d

    def kernel(
        block_hbm, input_hbm, qkv_ref, wo_ref, in_ref, hidden_ref, small_ref, counts_ref, load_ref,
        block_out, input_grad, gain, shift, qkv, attn_bias, wo, in_grad, in_bias, hidden, out_bias, counts, loads,
        block_buffer, input_buffer, here,
    ):
        copies = []
        for i in range(2 * PARTS):
            source, buffer, target = ((block_hbm, block_buffer, block_out), (input_hbm, input_buffer, input_grad))[i % 2]
            rows = pl.ds(i // 2 * (n // PARTS), n // PARTS)
            copies.append(
                (
                    pltpu.make_async_copy(source.at[rows], buffer.at[rows], here.at[2 * i]),
                    pltpu.make_async_copy(buffer.at[rows], target.at[rows], here.at[2 * i + 1]),
                )
            )
        for copy in copies:
            copy[0].start()
        for copy in copies:
            copy[0].wait()
            copy[1].start()
        core = lax.axis_index("core")
        chip = lax.axis_index("dp") * nx + lax.axis_index("xy")
        first = (chip * 2 + core) * share
        own = pltpu.roll(small_ref[...], lax.rem(d - first, d), axis=1)
        gain[...] = own[0:2, :share]
        shift[...] = own[2:4, :share]
        attn_bias[...] = own[4:7, :share]
        out_bias[...] = own[8:10, :share]
        cut = hidden_share // CUTS
        first = chip * cut
        rows = lax.broadcasted_iota(jnp.int32, small_ref.shape, 0)
        for expert in range(EXPERTS):
            for k in range(CUTS):
                start = k * (width // CUTS)
                row = 10 + (expert * CHUNKS + core) * lines + start // d
                line = jnp.sum(jnp.where(rows == row, small_ref[...], 0.0), axis=0, keepdims=True)
                line = pltpu.roll(jnp.broadcast_to(line, (8, d)), lax.rem(2 * d - start % d - first, d), axis=1)
                in_bias[expert : expert + 1, k * cut : (k + 1) * cut] = line[0:1, :cut]
        qkv[...] = qkv_ref[...].astype(F32)
        wo[...] = wo_ref[...].astype(F32)
        hidden[...] = hidden_ref[...].astype(F32)
        join_columns(in_ref, in_grad, hidden_share)
        lane = lax.broadcasted_iota(jnp.int32, (1, 128), 1)
        digits = counts_ref[0:1, :]
        second = jnp.sum(jnp.where(lane == 0, digits * 32, jnp.where(lane == 1, digits, 0.0)))
        for expert, count in enumerate((n * devices - second, second)):
            counts[expert] = count.astype(jnp.int32)
            loads[expert] = 0.9 * load_ref[expert] + 0.1 * (count * (EXPERTS / (n * devices)))
        for copy in copies:
            copy[1].wait()

    def f32(*shape):
        return jax.ShapeDtypeStruct(shape, F32)

    scalars = pl.BlockSpec(memory_space=pltpu.SMEM)
    return pl.pallas_call(
        kernel,
        out_shape=[
            jax.ShapeDtypeStruct((n, d), BF16),
            f32(n, d),
            f32(2, share),
            f32(2, share),
            f32(depth, 3 * d),
            f32(3, share),
            f32(depth, d),
            f32(EXPERTS, depth, CHUNKS * width),
            f32(EXPERTS, hidden_share),
            f32(EXPERTS, hidden_share, d),
            f32(EXPERTS, share),
            jax.ShapeDtypeStruct((EXPERTS,), jnp.int32),
            f32(EXPERTS),
        ],
        in_specs=[HBM] * 2 + [VMEM] * 6 + [scalars],
        out_specs=[HBM] * 2 + [VMEM] * 9 + [scalars] * 2,
        scratch_shapes=[
            pltpu.VMEM((n, d), BF16),
            pltpu.VMEM((n, d), F32),
            pltpu.SemaphoreType.DMA((4 * PARTS,)),
        ],
        compiler_params=pltpu.CompilerParams(vmem_limit_bytes=60 * MIB),
        name="results",
    )(
        block["block_out"], block["input_grad"], block["qkv_sum"], block["wo_sum"], block["in_sum"], block["hidden_sum"],
        block["small_sum"], block["counts"], running_load,
    )


def shards(
    nz, nx, tokens, norm_gain, norm_bias, w_qkv, attn_bias, w_attn_out, expert_in, expert_in_bias, expert_out,
    expert_out_bias, expert_ids, running_load, cotangent,
):
    chips = nz * nx
    depth, width = expert_in.shape[1:]
    share, hidden_share = norm_gain.shape[1], expert_out.shape[1]

    tiled = (EXPERTS, depth, CHUNKS, CUTS, chips, hidden_share // CUTS)
    if not whole_tiles(hidden_share):
        expert_in = expert_in.reshape(EXPERTS, depth, chips, CHUNKS, CUTS, -1).transpose(0, 1, 3, 4, 2, 5)
        expert_in = expert_in.reshape(EXPERTS, depth, width)
    small = (norm_gain, norm_bias, attn_bias, expert_out_bias, expert_in_bias)
    ids = expert_ids.reshape(1, tokens.shape[0])
    block = block_kernel(nz, nx, tokens, cotangent, ids, small, w_qkv, w_attn_out, expert_in, expert_out)
    results = list(result_kernel(nz, nx, block, running_load, share, hidden_share))
    if not whole_tiles(hidden_share):
        in_grad = results[7].reshape(tiled).transpose(0, 1, 4, 2, 3, 5)
        results[7] = in_grad.reshape(EXPERTS, depth, width)
    return tuple(results)


def solution(mesh):
    nz, nx = mesh.shape["dp"], mesh.shape["fsdp"] // 2
    fine = Mesh(mesh.devices.reshape(nz, nx, 2), ("dp", "xy", "core"))
    every = ("dp", "xy", "core")
    row, column, middle = P(every, None), P(None, every), P(None, every, None)
    return jax.shard_map(
        functools.partial(shards, nz, nx),
        mesh=fine,
        in_specs=(
            row, column, column, row, column, row, middle, column, middle, column, row, P(), row,
        ),
        out_specs=(row, row, column, column, row, column, row, middle, column, middle, column, P(), P()),
        check_vma=False,
    )
```

profile of v0, /device:TPU:0, one launch (start us, length us, event | category | flops | bytes accessed | tf_op | source)
XLA Modules:
  0.0 368.9 jit_solution(7039556000393909562)
XLA Ops:
  0.6 359.4 %block.1 = (bf16[1024,1024]{1,0:T(8,128)(2,1)}, f32[1024,1024]{1,0:T(8,128)}, bf16[32,3072]{1,0:T(8,128)(2,1)}, bf16[32,1024]{1,0:T(8,128)(2,1)}, bf16[2,2,32,20...) custom-call(bf16[1024,1024]{1,0:T(8,128)(2,1)} %refs_0_.1, ...), custom_call_target="tpu_custom_call" | custom-call | tf_op jit(solution)/shard_map/block/pallas_call | solution.py:1259
  360.1 8.5 %results.1 = (bf16[1024,1024]{1,0:T(8,128)(2,1)}, f32[1024,1024]{1,0:T(8,128)}, f32[2,32]{1,0:T(2,128)}, f32[2,32]{1,0:T(2,128)}, f32[32,3072]{1,0:T(8,128)}, /*...) custom-call(bf16[1024,1024]{1,0:T(8,128)(2,1)} %get-tuple-element.21, ...), custom_call_target="tpu_custom_call" | custom-call | tf_op jit(solution)/shard_map/results/pallas_call | solution.py:1351
where the time goes:
time: 374 us; the launch traced here: 369 us
  Pallas kernels  368 us (98%)
    pallas_call x1, Pallas kernels, block_kernel(): pl.pallas_call(kernel, out_shape=list(outputs.values()) + list(small_outp...  359 us
    pallas_call x1, Pallas kernels, result_kernel(): pl.pallas_call(kernel, out_shape=[jax.ShapeDtypeStruct((n, d), BF16), f32...  8.51 us

commit v1 on v0

--- a/solution.py
+++ b/solution.py
@@ -574,83 +574,78 @@
 
 
 PLAN_MESH = (4, 4)
-GATHER_ACROSS = (7, 11, 15, 17)
-REDUCE_ACROSS = (7, 8, 14)
+GATHER_ACROSS = (7, 9, 15, 17)
+REDUCE_ACROSS = (7, 8, 14, 16)
 PLAN = {
-    "s0": (0,),
-    "s1": (10, 70, 110, 170, 150,),
-    "s2": (1,),
-    "s3": (20, 71,),
-    "w0": (111, 171, 2, 11, 21, 151, 40, 12, 80, 3, 30, 41, 22, 81, 13, 31, 4, 50, 42, 90,),
-    "w1": (82, 60, 51, 23, 14, 91, 100,),
-    "w2": (43, 61, 120, 83, 101, 24, 72, 32,),
-    "q0": (52, 121, 92,),
-    "q1": (33, 112,),
-    "q3": (53,),
-    "h0": (73,),
-    "h1": (34, 93,),
-    "h2": (62,),
-    "h3": (102, 113,),
-    "h4": (122,),
-    "h5": (63,),
-    "h6": (103, 160,),
-    "h7": (130,),
-    "o0": (123, 161,),
-    "o1": (131,),
-    "o2": (140,),
-    "o3": (162, 180,),
-    "d0": (132, 172,),
-    "e0": (163,),
-    "t0.0": (133,),
-    "t1.0": (141,),
-    "t2.0": (181,),
-    "t0.1": (142, 173,),
-    "t1.1": (182,),
+    "s0": (0, 10,),
+    "s1": (20, 90, 70, 170, 150,),
+    "s2": (30,),
+    "s3": (40,),
+    "w0": (91, 71, 171, 151, 1, 80, 11, 21, 31, 2, 41, 12, 81, 3, 50, 60, 22, 100, 32, 42, 92, 82, 4, 13, 23, 51, 61,),
+    "q0.0": (33, 101, 93,),
+    "q0.3": (43,),
+    "w1": (14, 24, 83, 110, 120,),
+    "q1.0": (72,),
+    "q1.1": (52,),
+    "q1.3": (34, 62,),
+    "q2.1": (102,),
+    "h0": (111, 121,),
+    "h1": (160,),
+    "h2": (53, 63, 130, 140,),
+    "h3": (73,),
+    "h4": (103,),
+    "h5": (112,),
+    "h6": (122, 161,),
+    "h7": (131, 141,),
+    "o0": (180,),
+    "o1": (172,),
+    "o2": (113, 123,),
+    "d1": (162, 181,),
+    "e0": (132, 142, 190, 152,),
+    "t0.0": (182,),
+    "t0.1": (163, 133, 173,),
     "t2.1": (143,),
-    "t0.2": (183, 190,),
-    "t1.2": (152,),
+    "t0.2": (191,),
+    "t1.2": (183, 153,),
     "t2.2": (1000,),
-    "t1.3": (1040,),
-    "t2.3": (191,),
-    "t0.4": (153, 1001,),
-    "t1.4": (192,),
-    "t2.4": (1041,),
-    "t0.5": (193, 1002,),
-    "t1.5": (1042, 1010,),
-    "t2.5": (1070,),
+    "t1.3": (192,),
+    "t2.3": (1040,),
+    "t1.4": (1070,),
+    "t2.4": (1001, 1010,),
+    "t0.5": (193,),
+    "t1.5": (1080,),
+    "t2.5": (1041,),
     "t0.6": (1050,),
-    "t2.6": (1003, 1011,),
-    "t0.7": (1043, 1051,),
-    "t1.7": (1004, 1012, 1020,),
-    "t2.7": (1044, 1052, 1060,),
-    "x": (1071,),
-    "b0": (1021,),
-    "b1": (1013, 1061,),
-    "b2": (1053, 1030,),
-    "b3": (1014, 1022, 1072, 1120, 1062,),
-    "wo2": (1054, 1190, 1080,),
-    "a0": (1031,),
-    "a1": (1023, 1073, 1121,),
-    "a2": (1063, 1074, 1090,),
-    "a3": (1024, 1032, 1064, 1130,),
-    "a4": (1081, 1091,),
-    "a5": (1131,),
-    "a6": (1033, 1100,),
-    "a7": (1122, 1150,),
-    "free": (1034, 1092, 1082, 1132,),
-    "p0": (1123, 1101, 1160, 1110, 1140,),
-    "p1": (1170, 1191,),
-    "p2": (1124, 1180,),
-    "i0": (1093,),
-    "i1": (1083, 1133, 1111,),
-    "i2": (1192, 1102, 1084, 1094, 1151, 1141,),
-    "i3": (1134, 1161,),
-    "m0": (1171,),
-    "m1": (1193,),
-    "m2": (1103, 1142, 1162, 1112,),
-    "m3": (1194, 1172,),
-    "m4": (1104, 1143, 1113, 1181, 1152,),
-    "end": (1144, 1163, 1114, 1173, 1153, 1182, 1164, 1174, 1154, 1183, 1184,),
+    "t1.6": (1002, 1011,),
+    "e7": (1020, 1071,),
+    "t1.7": (1003,),
+    "t2.7": (1042, 1012, 1051, 1021, 1060,),
+    "x": (1081,),
+    "b0": (1004, 1030, 1072, 1043,),
+    "b1": (1013, 1061, 1120,),
+    "b2": (1052, 1022, 1073,),
+    "b3": (1044, 1031, 1082, 1090, 1014, 1140,),
+    "wo2": (1074, 1190,),
+    "a0": (1053, 1023, 1083, 1121, 1130,),
+    "a1": (1062, 1032, 1091, 1084, 1100, 1141,),
+    "a2": (1054, 1024,),
+    "a3": (1131, 1063, 1150,),
+    "a4": (1033, 1101, 1122, 1110,),
+    "a5": (1064, 1092,),
+    "a6": (1034, 1123, 1132, 1142, 1093, 1151,),
+    "a7": (1102, 1143, 1111,),
+    "p0": (1160, 1124, 1094, 1133, 1144, 1152,),
+    "p1": (1170, 1161, 1191,),
+    "p2": (1171, 1180, 1134,),
+    "i0": (1103,),
+    "i1": (1181, 1192, 1112, 1153,),
+    "i2": (1104, 1162, 1172,),
+    "m0": (1154,),
+    "m1": (1182, 1193, 1173,),
+    "m2": (1113,),
+    "m3": (1163, 1183,),
+    "m4": (1174, 1194,),
+    "end": (1164, 1114, 1184,),
 }
 
 
@@ -789,9 +784,9 @@
             return lambda zs, xs: [ref.at[zs, xs, core, :, pl.ds(part * d, d)]]
 
         def with_small(zs, xs):
-            return [out["qkv_full"].at[zs, xs, core, :, pl.ds(2 * d, d)], small_full.at[zs, xs, core]]
-
-        regions = [columns_of(out["qkv_full"], 0), columns_of(out["qkv_full"], 1), with_small, columns_of(out["wo_full"], 0)]
+            return [out["qkv_full"].at[zs, xs, core, :, pl.ds(0, d)], small_full.at[zs, xs, core]]
+
+        regions = [with_small, columns_of(out["qkv_full"], 1), columns_of(out["qkv_full"], 2), columns_of(out["wo_full"], 0)]
         gathered = [(order, region, region(ALL, ALL)) for order, region in zip(gather_order, regions)]
         for chunk in range(CHUNKS):
             for i in range(CUTS):
@@ -846,6 +841,9 @@
             loads = [load("qkv", qkv_own, qkv), load("wo", wo_own, wo), load("hidden", hidden_own, hidden)]
             load_shard = load("shard", in_shard, shard)
             load_cot = load("cot", cot_hbm, cot)
+            count_second = find_slots(slots, ids_ref, core)
+            pack_small(small_own, (gain_ref, shift_ref, attn_bias_ref, out_bias_ref, in_bias_ref), count_second)
+            small_full[z, xy, core] = small_own[...].astype(BF16)
             place.barrier()
             loads[0].wait()
             near = [load("own qkv", qkv, out["qkv_full"].at[z, xy, core])]
@@ -865,9 +863,6 @@
                 pair.append(made.far(("pair in", chunk), in_own.at[chunk, 1 - core], target, place.sibling()))
             for copy in pair:
                 copy.start()
-            count_second = find_slots(slots, ids_ref, core)
-            pack_small(small_own, (gain_ref, shift_ref, attn_bias_ref, out_bias_ref, in_bias_ref), count_second)
-            small_full[z, xy, core] = small_own[...].astype(BF16)
             for copy in late + pair:
                 copy.wait()
             schedule.at("s1")
@@ -897,29 +892,30 @@
         def forward_phase(tok, w, wo, normed, qkv, attended, logs, residual, normed_two, picked):
             load = made.local("tokens", tokens_hbm, tok)
             load.start()
-            loads = []
             for part in range(3):
                 schedule.need(f"w{part}", gather, [part])
                 at_columns = pl.ds(part * d, d)
-                loads.append(
-                    made.local(
-                        ("w", part), out["qkv_full"].at[:, :, :, :, at_columns], w.at[:, :, :, :, at_columns]
+                load_w = made.local(
+                    ("w", part), out["qkv_full"].at[:, :, :, :, at_columns], w.at[:, :, :, :, at_columns]
+                )
+                load_w.start()
+                if part == 0:
+                    unpack_small(
+                        small_full, core, d, share, hidden_share, vectors, in_bias, out_bias, out["counts"]
                     )
-                )
-                loads[-1].start()
-            unpack_small(small_full, core, d, share, hidden_share, vectors, in_bias, out_bias, out["counts"])
-            load.wait()
-            for copy in loads:
-                copy.wait()
-
-            @pl.loop(0, n // BLOCK)
-            def _(i):
-                rows = pl.ds(pl.multiple_of(i * BLOCK, BLOCK), BLOCK)
-                scaled, _ = row_stats(tok[rows].astype(F32))
-                normed[rows] = (scaled * vectors[0:1, :d] + vectors[1:2, :d]).astype(BF16)
-                weight = as_rows(w[...], d)
-                qkv[rows] = (dot(normed[rows], weight) + vectors[2:3, :]).astype(BF16)
-                schedule.in_loop(i, "q", n // BLOCK)
+                    load.wait()
+                load_w.wait()
+
+                @pl.loop(0, n // BLOCK)
+                def _(i, part=part):
+                    rows = pl.ds(pl.multiple_of(i * BLOCK, BLOCK), BLOCK)
+                    if part == 0:
+                        scaled, _ = row_stats(tok[rows].astype(F32))
+                        normed[rows] = (scaled * vectors[0:1, :d] + vectors[1:2, :d]).astype(BF16)
+                    columns = slice(part * d, (part + 1) * d)
+                    weight = as_rows(w[:, :, :, :, columns], d)
+                    qkv[rows, columns] = (dot(normed[rows], weight) + vectors[2:3, columns]).astype(BF16)
+                    schedule.in_loop(i, f"q{part}.", n // BLOCK)
 
             saves = [
                 made.local("save normed", normed, out["normed"]),

time: 374 us -> 366 us (0.979)
  Pallas kernels: 368 us -> 362 us
    pallas_call x1, Pallas kernels: 359 us -> 353 us  [block_kernel(): pl.pallas_call(kernel, out_shape=list(outputs.values()) + list(small_outp...]
where the time goes in v1:
time: 366 us; the launch traced here: 363 us
  Pallas kernels  362 us (99%)
    pallas_call x1, Pallas kernels, block_kernel(): pl.pallas_call(kernel, out_shape=list(outputs.values()) + list(small_outp...  353 us
    pallas_call x1, Pallas kernels, result_kernel(): pl.pallas_call(kernel, out_shape=[jax.ShapeDtypeStruct((n, d), BF16), f32...  8.51 us

profile of v1, /device:TPU:0, one launch (start us, length us, event | category | flops | bytes accessed | tf_op | source)
XLA Modules:
  0.0 362.7 jit_solution(17981622283404645895)
XLA Ops:
  0.6 353.2 %block.1 = (bf16[1024,1024]{1,0:T(8,128)(2,1)}, f32[1024,1024]{1,0:T(8,128)}, bf16[32,3072]{1,0:T(8,128)(2,1)}, bf16[32,1024]{1,0:T(8,128)(2,1)}, bf16[2,2,32,20...) custom-call(bf16[1024,1024]{1,0:T(8,128)(2,1)} %refs_0_.1, ...), custom_call_target="tpu_custom_call" | custom-call | tf_op jit(solution)/shard_map/block/pallas_call | solution.py:1255
  353.9 8.5 %results.1 = (bf16[1024,1024]{1,0:T(8,128)(2,1)}, f32[1024,1024]{1,0:T(8,128)}, f32[2,32]{1,0:T(2,128)}, f32[2,32]{1,0:T(2,128)}, f32[32,3072]{1,0:T(8,128)}, /*...) custom-call(bf16[1024,1024]{1,0:T(8,128)(2,1)} %get-tuple-element.21, ...), custom_call_target="tpu_custom_call" | custom-call | tf_op jit(solution)/shard_map/results/pallas_call | solution.py:1347
